TPU v7x, 128 devices: a whole 4x4x4 slice. The times are simulated.
128 devices in a mesh: dp: 16 (over x, z_hi, core), tensor: 8 (over y, z_lo).
Axes of the slice: x: 4, y: 4, z: 4 (z_hi: 2, z_lo: 2; z = z_hi * 2 + z_lo), core: 2. Of those that a mesh axis runs over, the one named last changes fastest.
Arguments:
- gate_pre: bfloat16 [16384, 14336], P('dp', 'tensor'), may hold values from -6 to 6
- up_pre: bfloat16 [16384, 14336], P('dp', 'tensor'), may hold values from -6 to 6
- out_grad: bfloat16 [16384, 4096], P(('dp', 'tensor')), may hold values from -6 to 6
- w_blocks: bfloat16 [8, 16, 26, 128, 128], P('tensor', 'dp'), may hold values from -0.0625 to 0.0625
- block_ids: int32 [8, 16, 26], P('tensor', 'dp'), may hold values from 0 to 448, as said below
Outputs:
- mixed: bfloat16 [16384, 4096], P(('dp', 'tensor'))
- gate_grad: bfloat16 [16384, 14336], P('dp', 'tensor')
- up_grad: bfloat16 [16384, 14336], P('dp', 'tensor')
- block_grads: float32 [8, 16, 26, 128, 128], P('tensor', 'dp')
Inputs may be any that keep to these rules, and one draw needn't show every extreme that they name: block_ids[t, o, s] is r * 32 + c for a nonzero block (r, c) of slice t's 14 x 32 block grid, or 448 for an empty slot; each nonzero block of a slice is listed exactly once among its owners; each block row holds exactly 16 nonzero blocks and each block column exactly 7; in every slice one owner fills all 26 slots.
All inputs are finite; a program needn't handle non-finite values.
Results may differ from a plain program's by a relative error of at most 0.017.
Values may be sent and summed in bfloat16 or wider, within the bound.
A program may use at most 192 MiB of HBM per device.

v0:
```python
import math

import jax
import jax.numpy as jnp
from jax import lax
from jax.sharding import PartitionSpec as P


def block_orders(block_list, row_blocks, column_blocks):
    block_total = row_blocks * column_blocks
    slot_count = block_list.shape[0]
    matches = (block_list[None, :] == jnp.arange(block_total, dtype=jnp.int32)[:, None]).astype(
        jnp.int32
    )
    present = jnp.sum(matches, axis=1, dtype=jnp.int32).reshape(row_blocks, column_blocks)
    slot_index = jnp.sum(
        matches * jnp.arange(slot_count, dtype=jnp.int32)[None, :], axis=1, dtype=jnp.int32
    ).reshape(row_blocks, column_blocks)
    rank_column = jnp.cumsum(present, axis=0, dtype=jnp.int32) - 1
    rank_row = jnp.cumsum(present, axis=1, dtype=jnp.int32) - 1
    column_pick = (present[:, :, None] == 1) & (
        rank_column[:, :, None] == jnp.arange(row_blocks // 2, dtype=jnp.int32)[None, None, :]
    )
    column_rows = jnp.sum(
        column_pick.astype(jnp.int32) * jnp.arange(row_blocks, dtype=jnp.int32)[:, None, None],
        axis=0,
        dtype=jnp.int32,
    )
    row_pick = (present[:, :, None] == 1) & (
        rank_row[:, :, None] == jnp.arange(column_blocks // 2, dtype=jnp.int32)[None, None, :]
    )
    row_columns = jnp.sum(
        row_pick.astype(jnp.int32) * jnp.arange(column_blocks, dtype=jnp.int32)[None, :, None],
        axis=1,
        dtype=jnp.int32,
    )
    column_slots = slot_index[column_rows, jnp.arange(column_blocks, dtype=jnp.int32)[:, None]]
    row_slots = slot_index[jnp.arange(row_blocks, dtype=jnp.int32)[:, None], row_columns]
    return (column_rows, row_columns, rank_column, column_slots, row_slots)


def pick_blocks(source, block_list, rank_column, row_blocks, column_blocks):
    is_used = block_list < row_blocks * column_blocks
    row_index = jnp.where(is_used, block_list // column_blocks, 0).astype(jnp.int32)
    column_index = jnp.where(is_used, block_list % column_blocks, 0).astype(jnp.int32)
    rank_index = jnp.maximum(rank_column[row_index, column_index], 0)
    return source[column_index, rank_index] * is_used.astype(source.dtype)[:, None, None]


def gated(gate_rows, up_rows):
    gate_value = gate_rows.astype(jnp.float32)
    return (jax.nn.silu(gate_value) * up_rows.astype(jnp.float32)).astype(jnp.bfloat16)


def input_grads(grad_hidden, gate_rows, up_rows):
    gate_value = gate_rows.astype(jnp.float32)
    up_value = up_rows.astype(jnp.float32)
    sigmoid_gate = jax.nn.sigmoid(gate_value)
    gate_grad = grad_hidden * up_value * sigmoid_gate * (1.0 + gate_value * (1.0 - sigmoid_gate))
    up_grad = grad_hidden * gate_value * sigmoid_gate
    return (gate_grad.astype(jnp.bfloat16), up_grad.astype(jnp.bfloat16))


def block_major(rows_array, block_size):
    row_count = rows_array.shape[0]
    return jnp.swapaxes(rows_array.reshape(row_count, -1, block_size), 0, 1)


def forward_rows(hidden_rows, by_column, column_rows):
    row_count = hidden_rows.shape[0]
    block_size = by_column.shape[-1]
    hidden_major = block_major(hidden_rows, block_size)
    column_count, rank_count = column_rows.shape

    def forward_add_rank(rank, total):
        picks = lax.dynamic_index_in_dim(column_rows, rank, 1, keepdims=False)
        panel = jnp.take(hidden_major, picks, axis=0)
        weight_rank = lax.dynamic_index_in_dim(by_column, rank, 1, keepdims=False)
        return total + jnp.einsum(
            "cta,cad->ctd", panel, weight_rank, preferred_element_type=jnp.float32
        )

    initial = jnp.zeros((column_count, row_count, block_size), jnp.float32)
    total = lax.fori_loop(0, rank_count, forward_add_rank, initial)
    return jnp.swapaxes(total, 0, 1).reshape(row_count, -1)


def backward_rows(grad_rows, by_row, row_columns):
    row_count = grad_rows.shape[0]
    block_size = by_row.shape[-1]
    grad_major = block_major(grad_rows, block_size)
    row_block_count, rank_count = row_columns.shape

    def backward_add_rank(rank, total):
        picks = lax.dynamic_index_in_dim(row_columns, rank, 1, keepdims=False)
        panel = jnp.take(grad_major, picks, axis=0)
        weight_rank = lax.dynamic_index_in_dim(by_row, rank, 1, keepdims=False)
        return total + jnp.einsum(
            "rtd,rkd->rtk", panel, weight_rank, preferred_element_type=jnp.float32
        )

    initial = jnp.zeros((row_block_count, row_count, block_size), jnp.float32)
    total = lax.fori_loop(0, rank_count, backward_add_rank, initial)
    return jnp.swapaxes(total, 0, 1).reshape(row_count, -1)


def weight_rows(hidden_rows, grad_rows, column_rows, block_size):
    hidden_major = block_major(hidden_rows, block_size)
    grad_major = block_major(grad_rows, block_size)

    def one_rank(carry, picks):
        panel = jnp.take(hidden_major, picks, axis=0)
        return (
            carry,
            jnp.einsum("cta,ctd->cad", panel, grad_major, preferred_element_type=jnp.float32),
        )

    unused, stacked = lax.scan(
        one_rank, jnp.zeros((), jnp.float32), jnp.swapaxes(column_rows, 0, 1)
    )
    return jnp.swapaxes(stacked, 0, 1)


def block_rows(row_count):
    step_rows = math.gcd(row_count, 256)
    return step_rows


def blockwise_map(func, inputs):
    row_count = inputs[0].shape[0]
    step_rows = block_rows(row_count)
    pieces = tuple(
        (
            member.reshape((row_count // step_rows, step_rows) + member.shape[1:])
            for member in inputs
        )
    )
    result = lax.map(lambda grouped: func(*grouped), pieces)
    return jax.tree.map(lambda output: output.reshape((row_count,) + output.shape[2:]), result)


def blockwise_sum(func, inputs, initial):
    row_count = inputs[0].shape[0]
    step_rows = block_rows(row_count)
    pieces = tuple(
        (
            member.reshape((row_count // step_rows, step_rows) + member.shape[1:])
            for member in inputs
        )
    )
    summed, unused = lax.scan(
        lambda running, grouped: (running + func(*grouped), None), initial, pieces
    )
    return summed


def local(gate_pre, up_pre, out_grad, w_blocks, block_ids):
    block_size = w_blocks.shape[-1]
    row_blocks = gate_pre.shape[1] // block_size
    column_blocks = out_grad.shape[1] // block_size
    group_rows = gate_pre.shape[0]
    grad_scale = 1.0 / math.sqrt(group_rows * lax.axis_size("dp"))
    gathered, gathered_ids = (
        lax.all_gather(w_blocks[0, 0], "dp", axis=0, tiled=True),
        lax.all_gather(block_ids[0, 0], "dp", axis=0, tiled=True),
    )
    column_rows, row_columns, rank_column, column_slots, row_slots = block_orders(
        gathered_ids, row_blocks, column_blocks
    )
    by_column = gathered[column_slots]
    by_row = gathered[row_slots]
    hidden = gated(gate_pre, up_pre)

    def forward_part(hidden_rows):
        return forward_rows(hidden_rows, by_column, column_rows)

    mixed = lax.psum_scatter(
        blockwise_map(forward_part, (hidden,)).astype(jnp.bfloat16),
        "tensor",
        scatter_dimension=0,
        tiled=True,
    )

    def input_part(grad_rows, gate_rows, up_rows):
        return input_grads(backward_rows(grad_rows, by_row, row_columns), gate_rows, up_rows)

    def weight_part(hidden_rows, grad_rows):
        return weight_rows(hidden_rows, grad_rows, column_rows, block_size)

    zero_grad = jnp.zeros((column_blocks, row_blocks // 2, block_size, block_size), jnp.float32)
    piece = lax.all_gather(out_grad, "tensor", axis=0, tiled=True)
    summed = zero_grad
    hidden_rows = hidden
    gate_rows = gate_pre
    up_rows = up_pre
    summed = blockwise_sum(weight_part, (hidden_rows, piece), summed)
    gate_piece, up_piece = blockwise_map(input_part, (piece, gate_rows, up_rows))
    gate_grad = gate_piece
    up_grad = up_piece
    summed, gate_grad, up_grad = (summed, gate_grad, up_grad)
    partial_grad = summed * grad_scale
    packed = pick_blocks(partial_grad, gathered_ids, rank_column, row_blocks, column_blocks)
    owned = lax.psum_scatter(
        packed.astype(jnp.bfloat16), "dp", scatter_dimension=0, tiled=True
    ).astype(jnp.float32)
    block_grads = owned[None, None]
    return (mixed, gate_grad, up_grad, block_grads)


def solution(mesh):
    placed = (
        P("dp", "tensor"),
        P("dp", "tensor"),
        P(("dp", "tensor"), None),
        P("tensor", "dp", None, None, None),
        P("tensor", "dp", None),
    )
    return jax.shard_map(
        local,
        mesh=mesh,
        in_specs=placed,
        out_specs=(
            P(("dp", "tensor"), None),
            P("dp", "tensor"),
            P("dp", "tensor"),
            P("tensor", "dp", None, None, None),
        ),
        check_vma=False,
    )
```

profile of v0, /device:TPU:1, one launch (start us, length us, event | category | flops | bytes accessed | tf_op | source)
XLA Modules:
  0.0 1148.6 jit_solution(10190954944929249618)
XLA Ops:
  11.4 13.1 %all-reduce = s32[416]{0:T(512)S(1)} all-reduce(s32[416]{0:T(512)S(1)} %bitcast_dynamic-update-slice_fusion.1), channel_id=2, replica_groups=mesh['dp'=16,'tensor'=8] {'dp'}, use_global_device_ids=true, to_apply=%add | all-reduce | flops 416 | bytes 3328 | tf_op jit(solution)/shard_map/all_gather | solution.py:165
  36.6 5.6 fusion.34
  42.2 6.0 copy.80
  48.1 133.1 %all-gather.5.cloned.1.call-done = bf16[1024,4096]{1,0:T(8,128)(2,1)} async-done(((bf16[128,4096]{1,0:T(8,128)(2,1)}), bf16[1024,4096]{1,0:T(8,128)(2,1)}) %all-gather.5.cloned.1.call-update) | async-done | bytes 8388624 | tf_op jit(solution)/shard_map/all_gather | solution.py:191
  181.3 11.9 %copy.82 = bf16[4,256,4096]{1,2,0:T(8,128)(2,1)} copy(bf16[4,256,4096]{2,1,0:T(8,128)(2,1)} %bitcast.115) | data formatting | bytes 16777216 | tf_op jit(solution)/shard_map/while | solution.py:138
  193.2 215.7 %while.77 = (s32[]{:T(128)}, f32[32,7,128,128]{3,2,0,1:T(8,128)}, s32[32,7]{0,1:T(8,128)S(1)}, bf16[4,256,1792]{1,2,0:T(8,128)(2,1)}, bf16[4,256,4096]{1,2,0:T(8,128)(2,1)}, /*index=5*/s32[]{:T(128)}, s32[]{:T(128)}, s32[]{:T(128)}) while((s32[]{:T(128)}, f32[32,7,128,128]{3,2,0,1:T(8,128)}, s32[32,7]{0,1:T(8,128)S(1)}, ...), condition=%wide.region_18.20_spmd.clone, body=%wide.region_15.19_spmd.clone.sunk | while | flops 276825280 | bytes 66589496 | solution.py:151
  199.7 33.4 %while.80 = (s32[]{:T(128)}, f32[7,32,128,128]{3,2,1,0:T(8,128)}, s32[7,32]{1,0:T(8,128)S(1)}, bf16[14,256,128]{2,1,0:T(8,128)(2,1)S(1)}, bf16[32,256,128]{2,1,0:T(8,128)(2,1)}, /*index=5*/s32[]{:T(128)}) while((s32[]{:T(128)}, f32[7,32,128,128]{3,2,1,0:T(8,128)}, s32[7,32]{1,0:T(8,128)S(1)}, bf16[14,256,128]{2,1,0:T(8,128)(2,1)S(1)}, ...), condition=%wide.region_17.18_spmd, body=%wide.region_16.17_spmd.sunk | while | flops 269485248 | bytes 10490517 | solution.py:118
  233.1 11.6 %bitcast_add_fusion.2 = f32[32,7,128,128]{3,2,0,1:T(8,128)} fusion(f32[7,32,128,128]{3,2,1,0:T(8,128)} %get-tuple-element.826, f32[32,7,128,128]{3,2,0,1:T(8,128)} %get-tuple-element.981, pred[]{:T(512)S(6)} %compare.12), kind=kLoop, calls=%fused_computation.60.clone.1 | loop fusion | flops 7340032 | bytes 44040192 | tf_op jit(solution)/shard_map/while/body/eval_jaxpr/add | solution.py:152
  251.2 33.6 %while.80 = (s32[]{:T(128)}, f32[7,32,128,128]{3,2,1,0:T(8,128)}, s32[7,32]{1,0:T(8,128)S(1)}, bf16[14,256,128]{2,1,0:T(8,128)(2,1)S(1)}, bf16[32,256,128]{2,1,0:T(8,128)(2,1)}, /*index=5*/s32[]{:T(128)}) while((s32[]{:T(128)}, f32[7,32,128,128]{3,2,1,0:T(8,128)}, s32[7,32]{1,0:T(8,128)S(1)}, bf16[14,256,128]{2,1,0:T(8,128)(2,1)S(1)}, ...), condition=%wide.region_17.18_spmd, body=%wide.region_16.17_spmd.sunk | while | flops 269485248 | bytes 10490517 | solution.py:118
  275.9 4.0 bitcast_dynamic-update-slice_fusion.3
  284.8 14.9 %bitcast_add_fusion.2 = f32[32,7,128,128]{3,2,0,1:T(8,128)} fusion(f32[7,32,128,128]{3,2,1,0:T(8,128)} %get-tuple-element.826, f32[32,7,128,128]{3,2,0,1:T(8,128)} %get-tuple-element.981, pred[]{:T(512)S(6)} %compare.12), kind=kLoop, calls=%fused_computation.60.clone.1 | loop fusion | flops 7340032 | bytes 44040192 | tf_op jit(solution)/shard_map/while/body/eval_jaxpr/add | solution.py:152
  306.2 33.2 %while.80 = (s32[]{:T(128)}, f32[7,32,128,128]{3,2,1,0:T(8,128)}, s32[7,32]{1,0:T(8,128)S(1)}, bf16[14,256,128]{2,1,0:T(8,128)(2,1)S(1)}, bf16[32,256,128]{2,1,0:T(8,128)(2,1)}, /*index=5*/s32[]{:T(128)}) while((s32[]{:T(128)}, f32[7,32,128,128]{3,2,1,0:T(8,128)}, s32[7,32]{1,0:T(8,128)S(1)}, bf16[14,256,128]{2,1,0:T(8,128)(2,1)S(1)}, ...), condition=%wide.region_17.18_spmd, body=%wide.region_16.17_spmd.sunk | while | flops 269485248 | bytes 10490517 | solution.py:118
  339.4 14.9 %bitcast_add_fusion.2 = f32[32,7,128,128]{3,2,0,1:T(8,128)} fusion(f32[7,32,128,128]{3,2,1,0:T(8,128)} %get-tuple-element.826, f32[32,7,128,128]{3,2,0,1:T(8,128)} %get-tuple-element.981, pred[]{:T(512)S(6)} %compare.12), kind=kLoop, calls=%fused_computation.60.clone.1 | loop fusion | flops 7340032 | bytes 44040192 | tf_op jit(solution)/shard_map/while/body/eval_jaxpr/add | solution.py:152
  360.8 33.2 %while.80 = (s32[]{:T(128)}, f32[7,32,128,128]{3,2,1,0:T(8,128)}, s32[7,32]{1,0:T(8,128)S(1)}, bf16[14,256,128]{2,1,0:T(8,128)(2,1)S(1)}, bf16[32,256,128]{2,1,0:T(8,128)(2,1)}, /*index=5*/s32[]{:T(128)}) while((s32[]{:T(128)}, f32[7,32,128,128]{3,2,1,0:T(8,128)}, s32[7,32]{1,0:T(8,128)S(1)}, bf16[14,256,128]{2,1,0:T(8,128)(2,1)S(1)}, ...), condition=%wide.region_17.18_spmd, body=%wide.region_16.17_spmd.sunk | while | flops 269485248 | bytes 10490517 | solution.py:118
  394.1 14.9 %bitcast_add_fusion.2 = f32[32,7,128,128]{3,2,0,1:T(8,128)} fusion(f32[7,32,128,128]{3,2,1,0:T(8,128)} %get-tuple-element.826, f32[32,7,128,128]{3,2,0,1:T(8,128)} %get-tuple-element.981, pred[]{:T(512)S(6)} %compare.12), kind=kLoop, calls=%fused_computation.60.clone.1 | loop fusion | flops 7340032 | bytes 44040192 | tf_op jit(solution)/shard_map/while/body/eval_jaxpr/add | solution.py:152
  409.0 13.5 %broadcast_multiply_fusion = f32[32,7,128,128]{3,2,0,1:T(8,128)} fusion(f32[32,7,128,128]{3,2,0,1:T(8,128)} %get-tuple-element.320), kind=kLoop, calls=%fused_computation.70 | loop fusion | flops 3670016 | bytes 29360128 | tf_op jit(solution)/shard_map/mul | solution.py:201
  422.5 31.7 %gather_fusion.8 = f32[416,128,128]{2,1,0:T(8,128)} fusion(f32[32,7,128,128]{3,2,0,1:T(8,128)} %broadcast_multiply_fusion, s32[416]{0:T(512)S(1)} %copy-done.2), kind=kCustom, calls=%fused_computation.8 | custom fusion | bytes 54529280 | tf_op jit(solution)/shard_map/gather | solution.py:47
  454.2 16.2 %multiply_convert_fusion = bf16[416,128,128]{2,1,0:T(8,128)(2,1)} fusion(f32[416,128,128]{2,1,0:T(8,128)} %gather_fusion.8, f32[416]{0:T(512)S(1)} %copy-done.5), kind=kLoop, calls=%fused_computation.63 | loop fusion | flops 13631488 | bytes 40896128 | tf_op jit(solution)/shard_map/convert_element_type | solution.py:204
  471.1 13.6 %gather_fusion.4 = bf16[224,128,128]{2,1,0:T(8,128)(2,1)} fusion(bf16[416,128,128]{2,1,0:T(8,128)(2,1)} %bitcast.111, s32[1024]{0:T(1024)S(1)} %copy-done.3), kind=kCustom, calls=%fused_computation.4 | custom fusion | bytes 14680960 | tf_op jit(solution)/shard_map/gather | solution.py:170
  484.6 15.4 %gather_fusion.6 = bf16[224,128,128]{2,1,0:T(8,128)(2,1)} fusion(bf16[416,128,128]{2,1,0:T(8,128)(2,1)} %bitcast.112, s32[1024]{0:T(1024)S(1)} %copy-done.4), kind=kCustom, calls=%fused_computation.6 | custom fusion | bytes 14680960 | tf_op jit(solution)/shard_map/gather | solution.py:171
  500.0 10.5 copy.84
  510.6 6.5 copy.81
  517.1 217.7 %while.73 = (s32[]{:T(128)}, bf16[4,256,4096]{2,1,0:T(8,128)(2,1)}, bf16[4,256,1792]{1,2,0:T(8,128)(2,1)}, s32[32,7]{0,1:T(8,128)S(1)}, bf16[32,7,128,128]{3,2,0...) while((s32[]{:T(128)}, bf16[4,256,4096]{2,1,0:T(8,128)(2,1)}, ...), condition=%wide.region_7.9_spmd, body=%wide.region_4.8_spmd.sunk | while | flops 271582400 | bytes 34083668 | solution.py:138
  519.2 42.6 %while.78 = (s32[]{:T(128)}, f32[32,256,128]{2,1,0:T(8,128)}, s32[32,7]{0,1:T(8,128)S(1)}, bf16[14,256,128]{2,1,0:T(8,128)(2,1)S(1)}, bf16[32,7,128,128]{3,2,0,1:T(8,128)(2,1)}, /*index=5*/s32[]{:T(128)}, s32[]{:T(128)}) while((s32[]{:T(128)}, f32[32,256,128]{2,1,0:T(8,128)}, s32[32,7]{0,1:T(8,128)S(1)}, ...), condition=%wide.region_6.7_spmd.clone, body=%wide.region_5.6_spmd.clone.sunk | while | flops 271582400 | bytes 15733415 | solution.py:84
  525.1 5.3 select_add_fusion.5
  531.4 5.2 select_add_fusion.5
  537.6 5.3 select_add_fusion.5
  543.9 5.3 select_add_fusion.5
  550.2 5.4 select_add_fusion.5
  556.5 5.2 select_add_fusion.5
  561.8 4.6 copy.109
  573.7 42.6 %while.78 = (s32[]{:T(128)}, f32[32,256,128]{2,1,0:T(8,128)}, s32[32,7]{0,1:T(8,128)S(1)}, bf16[14,256,128]{2,1,0:T(8,128)(2,1)S(1)}, bf16[32,7,128,128]{3,2,0,1:T(8,128)(2,1)}, /*index=5*/s32[]{:T(128)}, s32[]{:T(128)}) while((s32[]{:T(128)}, f32[32,256,128]{2,1,0:T(8,128)}, s32[32,7]{0,1:T(8,128)S(1)}, ...), condition=%wide.region_6.7_spmd.clone, body=%wide.region_5.6_spmd.clone.sunk | while | flops 271582400 | bytes 15733415 | solution.py:84
  579.6 5.4 select_add_fusion.5
  586.0 5.3 select_add_fusion.5
  592.3 5.3 select_add_fusion.5
  598.6 5.3 select_add_fusion.5
  604.9 5.2 select_add_fusion.5
  611.1 5.2 select_add_fusion.5
  616.3 4.6 copy.109
  628.3 42.2 %while.78 = (s32[]{:T(128)}, f32[32,256,128]{2,1,0:T(8,128)}, s32[32,7]{0,1:T(8,128)S(1)}, bf16[14,256,128]{2,1,0:T(8,128)(2,1)S(1)}, bf16[32,7,128,128]{3,2,0,1:T(8,128)(2,1)}, /*index=5*/s32[]{:T(128)}, s32[]{:T(128)}) while((s32[]{:T(128)}, f32[32,256,128]{2,1,0:T(8,128)}, s32[32,7]{0,1:T(8,128)S(1)}, ...), condition=%wide.region_6.7_spmd.clone, body=%wide.region_5.6_spmd.clone.sunk | while | flops 271582400 | bytes 15733415 | solution.py:84
  634.2 5.2 select_add_fusion.5
  640.4 5.2 select_add_fusion.5
  646.6 5.2 select_add_fusion.5
  652.8 5.2 select_add_fusion.5
  659.0 5.2 select_add_fusion.5
  665.3 5.2 select_add_fusion.5
  670.5 4.6 copy.109
  682.4 42.2 %while.78 = (s32[]{:T(128)}, f32[32,256,128]{2,1,0:T(8,128)}, s32[32,7]{0,1:T(8,128)S(1)}, bf16[14,256,128]{2,1,0:T(8,128)(2,1)S(1)}, bf16[32,7,128,128]{3,2,0,1:T(8,128)(2,1)}, /*index=5*/s32[]{:T(128)}, s32[]{:T(128)}) while((s32[]{:T(128)}, f32[32,256,128]{2,1,0:T(8,128)}, s32[32,7]{0,1:T(8,128)S(1)}, ...), condition=%wide.region_6.7_spmd.clone, body=%wide.region_5.6_spmd.clone.sunk | while | flops 271582400 | bytes 15733415 | solution.py:84
  688.4 5.2 select_add_fusion.5
  694.6 5.2 select_add_fusion.5
  700.8 5.2 select_add_fusion.5
  707.0 5.2 select_add_fusion.5
  713.2 5.2 select_add_fusion.5
  719.4 5.2 select_add_fusion.5
  724.7 4.6 copy.109
  734.8 404.7 %while.75 = (s32[]{:T(128)}, bf16[4,256,1792]{2,1,0:T(8,128)(2,1)}, bf16[4,256,1792]{2,1,0:T(8,128)(2,1)}, bf16[4,256,4096]{1,2,0:T(8,128)(2,1)}, s32[14,16]{0,1...) while((s32[]{:T(128)}, bf16[4,256,1792]{2,1,0:T(8,128)(2,1)}, ...), condition=%wide.region_14.16_spmd, body=%wide.region_11.15_spmd.sunk | while | flops 125699160 | bytes 42799692 | solution.py:138
  742.9 4.1 copy.112
  747.0 80.7 %while.79 = (s32[]{:T(128)}, f32[14,256,128]{2,1,0:T(8,128)S(1)}, s32[14,16]{0,1:T(8,128)}, bf16[32,256,128]{2,1,0:T(8,128)(2,1)}, bf16[14,16,128,128]{3,2,0,1:T(8,128)(2,1)}, /*index=5*/s32[]{:T(128)}, s32[]{:T(128)}) while((s32[]{:T(128)}, f32[14,256,128]{2,1,0:T(8,128)S(1)}, s32[14,16]{0,1:T(8,128)}, ...), condition=%wide.region_13.14_spmd.clone, body=%wide.region_12.13_spmd.clone.sunk | while | flops 118817880 | bytes 6885731 | solution.py:103
  844.6 4.1 copy.112
  848.7 80.1 %while.79 = (s32[]{:T(128)}, f32[14,256,128]{2,1,0:T(8,128)S(1)}, s32[14,16]{0,1:T(8,128)}, bf16[32,256,128]{2,1,0:T(8,128)(2,1)}, bf16[14,16,128,128]{3,2,0,1:T(8,128)(2,1)}, /*index=5*/s32[]{:T(128)}, s32[]{:T(128)}) while((s32[]{:T(128)}, f32[14,256,128]{2,1,0:T(8,128)S(1)}, s32[14,16]{0,1:T(8,128)}, ...), condition=%wide.region_13.14_spmd.clone, body=%wide.region_12.13_spmd.clone.sunk | while | flops 118817880 | bytes 6885731 | solution.py:103
  945.7 4.1 copy.112
  949.8 79.9 %while.79 = (s32[]{:T(128)}, f32[14,256,128]{2,1,0:T(8,128)S(1)}, s32[14,16]{0,1:T(8,128)}, bf16[32,256,128]{2,1,0:T(8,128)(2,1)}, bf16[14,16,128,128]{3,2,0,1:T(8,128)(2,1)}, /*index=5*/s32[]{:T(128)}, s32[]{:T(128)}) while((s32[]{:T(128)}, f32[14,256,128]{2,1,0:T(8,128)S(1)}, s32[14,16]{0,1:T(8,128)}, ...), condition=%wide.region_13.14_spmd.clone, body=%wide.region_12.13_spmd.clone.sunk | while | flops 118817880 | bytes 6885731 | solution.py:103
  1046.7 4.1 copy.112
  1050.7 79.9 %while.79 = (s32[]{:T(128)}, f32[14,256,128]{2,1,0:T(8,128)S(1)}, s32[14,16]{0,1:T(8,128)}, bf16[32,256,128]{2,1,0:T(8,128)(2,1)}, bf16[14,16,128,128]{3,2,0,1:T(8,128)(2,1)}, /*index=5*/s32[]{:T(128)}, s32[]{:T(128)}) while((s32[]{:T(128)}, f32[14,256,128]{2,1,0:T(8,128)S(1)}, s32[14,16]{0,1:T(8,128)}, ...), condition=%wide.region_13.14_spmd.clone, body=%wide.region_12.13_spmd.clone.sunk | while | flops 118817880 | bytes 6885731 | solution.py:103
  (608 shorter events, 631.9 us)
Async XLA Ops:
  7.2 174.1 %all-gather.5.cloned.1.call-start = ((), (), s32[]{:S(2)}) async-start(), calls=%async_computation.3 | async-start | bytes 9437184 | tf_op jit(solution)/shard_map/all_gather | solution.py:191
  7.9 462.6 %all-gather.7.cloned.1.call-start = ((), (), s32[]{:S(2)}) async-start(), calls=%async_computation.5 | async-start | bytes 14483456 | tf_op jit(solution)/shard_map/all_gather | solution.py:164
  8.6 1130.8 %reduce-scatter.5.cloned.1.call-start = ((), (), s32[]{:S(2)}) async-start(), calls=%async_computation.4 | async-start | bytes 14483456 | tf_op jit(solution)/shard_map/reduce_scatter | solution.py:203
  409.0 13.5 %copy-start.2 = (s32[416]{0:T(512)S(1)}, s32[416]{0:T(512)}, u32[]{:S(2)}) copy-start(s32[416]{0:T(512)} %shift-left_or_fusion) | copy-start | bytes 4996
  422.5 31.7 %copy-start.5 = (f32[416]{0:T(512)S(1)}, f32[416]{0:T(512)}, u32[]{:S(2)}) copy-start(f32[416]{0:T(512)} %fusion.48) | copy-start | bytes 4996
  470.4 0.7 copy-start.3
  470.4 671.6 %reduce-scatter.3.cloned.1.call-start = ((), (), s32[]{:S(2)}) async-start(), calls=%async_computation.2 | async-start | bytes 9437184 | tf_op jit(solution)/shard_map/reduce_scatter | solution.py:177
  471.1 13.6 %copy-start.4 = (s32[1024]{0:T(1024)S(1)}, s32[1024]{0:T(1024)}, u32[]{:S(2)}) copy-start(s32[1024]{0:T(1024)} %pad_clamp_fusion.3) | copy-start | bytes 12292
  500.0 10.5 copy-start.1
  827.6 1.8 copy-start
  928.8 1.8 copy-start
  1029.8 1.8 copy-start
  1130.7 1.8 copy-start
Sparse Core Ops, SparseCore 0:
  9.6 171.5 all-gather.4
  183.7 101.5 all-gather.6
  470.5 132.0 reduce-scatter.4
  734.9 173.7 reduce-scatter.2
where the time goes:
time: 1160 us; the launch traced here: 1150 us
  local copies, waits for them, and re-layouts  452 us (39%)
  matrix products  373 us (32%)
  other arithmetic  157 us (14%)
  waiting for transfers between devices  135 us (12%)
  between operations  14.6 us (1%)
  blocking collectives  13.1 us (1%)
    gather x64, local copies, waits for them, and re-layouts, backward_add_rank(): panel = jnp.take(grad_major, picks, axis=0)  149 us
    dot_general x28, matrix products, forward_add_rank(): jnp.einsum('cta,cad->ctd', panel, weight_rank, preferred_element_type=jnp...  142 us
    all_gather x1, waiting for transfers between devices, local(): piece = lax.all_gather(out_grad, 'tensor', axis=0, tiled=True)  133 us
    dot_general x64, matrix products, backward_add_rank(): jnp.einsum('rtd,rkd->rtk', panel, weight_rank, preferred_element_type=jnp...  125 us
    dot_general x28, matrix products, one_rank(): jnp.einsum('cta,ctd->cad', panel, grad_major, preferred_element_type=jnp....  106 us
    add x4, other arithmetic, blockwise_sum(): running + func(*grouped)  56.4 us
    reduce_and x64, other arithmetic, backward_add_rank(): panel = jnp.take(grad_major, picks, axis=0)  44.3 us
    while x5, local copies, waits for them, and re-layouts, blockwise_map(): result = lax.map(lambda grouped: func(*grouped), pieces)  35.6 us
  transfers between devices with their start and end apart: 4, of which 1 were waited for; matrix products, arithmetic and copies ran while one was open for 85% of the time, Pallas kernels for 0%

commit v1 on v0

v1 whole, which is shorter than its diff:
```python
import functools
import math

import jax
import jax.numpy as jnp
from jax import lax
from jax.experimental import pallas as pl
from jax.experimental.pallas import tpu as pltpu
from jax.sharding import PartitionSpec as P

MESH = pl.DeviceIdType.MESH
BF = jnp.bfloat16
F32 = jnp.float32
ANY = pl.BlockSpec(memory_space=pl.ANY)
VM = pl.BlockSpec(memory_space=pltpu.VMEM)
MIB = 1024 * 1024

N_DP = 16
N_T = 8
BLK = 128
TOK = 128
NFB = 14
NDB = 32
NLOC = NFB * NDB
MAXB = 26
D = NDB * BLK
HID = NFB * BLK
ROWS = TOK * N_T
PIECE = MAXB * BLK
META = 16
WROWS = PIECE + META
WHALF = 1680


def flip_core(i):
    return i + 1 - 2 * (i % 2)


def flip_far(i):
    return i + 2 - 4 * ((i // 2) % 2)


def greet(devices):
    barrier = pltpu.get_barrier_semaphore()
    for device in devices:
        pl.semaphore_signal(barrier, inc=1, device_id=device, device_id_type=MESH)
    pl.semaphore_wait(barrier, len(devices))


class Sends:
    def __init__(self, send, recv):
        self.send, self.recv, self.started = send, recv, []

    def start(self, i, src, dst, device):
        copy = pltpu.make_async_remote_copy(
            src, dst, self.send.at[i], self.recv.at[i], device_id=device, device_id_type=MESH
        )
        copy.start()
        self.started.append(copy)

    def arrived(self, i, dst, device):
        pltpu.make_async_remote_copy(
            dst, dst, self.send.at[i], self.recv.at[i], device_id=device, device_id_type=MESH
        ).wait_recv()

    def finish(self):
        for copy in self.started:
            copy.wait_send()


def gather_kernel(
    g_ref, w_ref, gate_ref, up_ref, g_all, w_all, h_out, ht_out,
    gate_v, up_v, h_v, ht_v, g_send, g_recv, w_send, w_recv, loc,
):
    dp, t = lax.axis_index("dp"), lax.axis_index("tensor")
    z, yp, ym, y2 = flip_core(t), (t + 2) % N_T, (t + 6) % N_T, (t + 4) % N_T
    h, xp, xm, x2 = flip_far(dp), (dp + 4) % N_DP, (dp + 12) % N_DP, (dp + 8) % N_DP
    c = flip_core(dp)
    Z, YP, YM = (dp, z), (dp, yp), (dp, ym)
    H, XP, XM, C = (h, t), (xp, t), (xm, t), (c, t)

    local = [
        pltpu.make_async_copy(gate_ref, gate_v, loc.at[0]),
        pltpu.make_async_copy(up_ref, up_v, loc.at[1]),
        pltpu.make_async_copy(g_ref, g_all.at[t], loc.at[2]),
        pltpu.make_async_copy(w_ref, w_all.at[dp], loc.at[3]),
    ]
    for copy in local:
        copy.start()
    greet((Z, YP, YM, H, XP, XM, C))

    g, w = Sends(g_send, g_recv), Sends(w_send, w_recv)
    lo, hi = pl.ds(0, TOK // 2), pl.ds(TOK // 2, TOK // 2)
    wlo, whi = pl.ds(0, WHALF), pl.ds(WHALF, WROWS - WHALF)

    g.start(0, g_ref, g_all.at[t], Z)
    w.start(0, w_ref, w_all.at[dp], H)
    g.start(1, g_ref, g_all.at[t], YP)
    g.start(2, g_ref, g_all.at[t], YM)
    w.start(1, w_ref, w_all.at[dp], XP)
    w.start(2, w_ref, w_all.at[dp], XM)
    w.start(9, w_ref, w_all.at[dp], C)

    local[0].wait()
    local[1].wait()

    @pl.loop(0, ROWS // TOK)
    def _(i):
        rows = pl.ds(pl.multiple_of(i * TOK, TOK), TOK)
        for b in range(NFB):
            cols = pl.ds(b * BLK, BLK)
            gate = gate_v[rows, cols].astype(F32)
            hid = (gate * jax.nn.sigmoid(gate) * up_v[rows, cols].astype(F32)).astype(BF)
            h_v[rows, cols] = hid
            ht_v[cols, rows] = hid.T

    outs = [
        pltpu.make_async_copy(h_v, h_out, loc.at[4]),
        pltpu.make_async_copy(ht_v, ht_out, loc.at[5]),
    ]
    for copy in outs:
        copy.start()

    w.arrived(1, w_all.at[xm], XM)
    w.start(5, w_all.at[xm, wlo], w_all.at[xm, wlo], XP)
    w.start(11, w_all.at[xm], w_all.at[xm], C)
    w.arrived(2, w_all.at[xp], XP)
    w.start(6, w_all.at[xp, whi], w_all.at[xp, whi], XM)
    w.start(12, w_all.at[xp], w_all.at[xp], C)

    g.arrived(0, g_all.at[z], Z)
    g.start(3, g_all.at[z], g_all.at[z], YP)
    g.start(4, g_all.at[z], g_all.at[z], YM)
    g.arrived(1, g_all.at[ym], YM)
    g.start(5, g_all.at[ym, lo], g_all.at[ym, lo], YP)
    g.arrived(2, g_all.at[yp], YP)
    g.start(6, g_all.at[yp, hi], g_all.at[yp, hi], YM)

    w.arrived(0, w_all.at[h], H)
    w.start(3, w_all.at[h], w_all.at[h], XP)
    w.start(4, w_all.at[h], w_all.at[h], XM)
    w.start(10, w_all.at[h], w_all.at[h], C)

    w.arrived(5, w_all.at[x2, wlo], XM)
    w.start(15, w_all.at[x2, wlo], w_all.at[x2, wlo], C)
    w.arrived(6, w_all.at[x2, whi], XP)
    w.start(16, w_all.at[x2, whi], w_all.at[x2, whi], C)

    zm, zp, z2 = flip_core(ym), flip_core(yp), flip_core(y2)
    g.arrived(3, g_all.at[zm], YM)
    g.start(7, g_all.at[zm, lo], g_all.at[zm, lo], YP)
    g.arrived(4, g_all.at[zp], YP)
    g.start(8, g_all.at[zp, hi], g_all.at[zp, hi], YM)

    hm, hp, h2 = flip_far(xm), flip_far(xp), flip_far(x2)
    w.arrived(3, w_all.at[hm], XM)
    w.start(7, w_all.at[hm, wlo], w_all.at[hm, wlo], XP)
    w.start(13, w_all.at[hm], w_all.at[hm], C)
    w.arrived(4, w_all.at[hp], XP)
    w.start(8, w_all.at[hp, whi], w_all.at[hp, whi], XM)
    w.start(14, w_all.at[hp], w_all.at[hp], C)
    w.arrived(7, w_all.at[h2, wlo], XM)
    w.start(17, w_all.at[h2, wlo], w_all.at[h2, wlo], C)
    w.arrived(8, w_all.at[h2, whi], XP)
    w.start(18, w_all.at[h2, whi], w_all.at[h2, whi], C)

    g.arrived(5, g_all.at[y2, lo], YM)
    g.arrived(6, g_all.at[y2, hi], YP)
    g.arrived(7, g_all.at[z2, lo], YM)
    g.arrived(8, g_all.at[z2, hi], YP)
    for i, source in ((9, dp), (10, h), (11, xm), (12, xp), (13, hm), (14, hp)):
        w.arrived(i, w_all.at[flip_core(source)], C)
    for i, source, part in ((15, x2, wlo), (16, x2, whi), (17, h2, wlo), (18, h2, whi)):
        w.arrived(i, w_all.at[flip_core(source), part], C)
    g.finish()
    w.finish()
    for copy in (local[2], local[3], outs[0], outs[1]):
        copy.wait()


def compute_kernel(
    scale, gate_ref, up_ref, h_ref, ht_ref, g_ref, w_ref, p_out, q_out, gg_out, ug_out,
    wd, h_v, ht_v, g_v, blocks, gate_v, up_v, meta_v, ids_v, ids_s, p_v, zero_v,
    loc, wsem, psem, qsem, osem,
):
    loads = [
        pltpu.make_async_copy(w_ref.at[:, pl.ds(PIECE, META)], meta_v, loc.at[0]),
        pltpu.make_async_copy(ht_ref, ht_v, loc.at[1]),
        pltpu.make_async_copy(g_ref, g_v, loc.at[2]),
        pltpu.make_async_copy(h_ref, h_v, loc.at[3]),
        pltpu.make_async_copy(gate_ref, gate_v, loc.at[4]),
        pltpu.make_async_copy(up_ref, up_v, loc.at[5]),
    ]
    for copy in loads:
        copy.start()

    @pl.loop(0, HID // 16)
    def _(i):
        wd[pl.ds(pl.multiple_of(i * 16, 16), 16), :] = jnp.zeros((16, D), BF)

    zero_v[...] = jnp.zeros((BLK, BLK), BF)
    loads[0].wait()
    for o in range(N_DP):
        both = meta_v[o].astype(F32)
        ids_v[o : o + 1, :] = (both[0:1, :] * NDB + both[1:2, :]).astype(jnp.int32)
    to_scalar = pltpu.make_async_copy(ids_v, ids_s, loc.at[6])
    to_scalar.start()
    to_scalar.wait()

    def place(o, s):
        b = ids_s[o, s]
        row = pl.multiple_of((b // NDB) * BLK, BLK)
        col = pl.multiple_of((b % NDB) * BLK, BLK)
        return b, row, col

    def w_copy(o, s):
        b, row, col = place(o, s)
        src = w_ref.at[o, pl.ds(pl.multiple_of(s * BLK, BLK), BLK), :]
        return b, pltpu.make_async_copy(src, wd.at[pl.ds(row, BLK), pl.ds(col, BLK)], wsem)

    @pl.loop(0, N_DP)
    def _(o):
        @pl.loop(0, MAXB)
        def _(s):
            b, copy = w_copy(o, s)

            @pl.when(b < NLOC)
            def _():
                copy.start()

    loads[1].wait()
    loads[2].wait()

    TN = 256

    @pl.loop(0, D // TN)
    def _(j):
        for i in range(2):
            rows = HID // 2
            cols = pl.ds(pl.multiple_of(j * TN, TN), TN)
            res = jnp.dot(ht_v[i * rows : (i + 1) * rows, :], g_v[:, cols], preferred_element_type=F32)
            res = (res * scale).astype(BF)
            for cb in range(TN // BLK):
                for rb in range(NFB // 2):
                    blocks[(j * (TN // BLK) + cb) * NFB + i * (NFB // 2) + rb] = res[
                        rb * BLK : (rb + 1) * BLK, cb * BLK : (cb + 1) * BLK
                    ]

    def q_copy(o, s, src):
        dst = q_out.at[o, pl.ds(pl.multiple_of(s * BLK, BLK), BLK), :]
        return pltpu.make_async_copy(src, dst, qsem)

    @pl.loop(0, N_DP)
    def _(o):
        @pl.loop(0, MAXB)
        def _(s):
            b = ids_s[o, s]

            @pl.when(b < NLOC)
            def _():
                q_copy(o, s, blocks.at[(b % NDB) * NFB + b // NDB]).start()

            @pl.when(b >= NLOC)
            def _():
                q_copy(o, s, zero_v).start()

    @pl.loop(0, N_DP)
    def _(o):
        @pl.loop(0, MAXB)
        def _(s):
            b, copy = w_copy(o, s)

            @pl.when(b < NLOC)
            def _():
                copy.wait()

    loads[3].wait()
    PN = 512

    def p_copy(j, slot):
        cols = pl.ds(pl.multiple_of(j * PN, PN), PN)
        return pltpu.make_async_copy(p_v.at[slot], p_out.at[:, cols], psem.at[slot])

    @pl.loop(0, D // PN)
    def _(j):
        slot = j % 2

        @pl.when(j >= 2)
        def _():
            p_copy(j - 2, slot).wait()

        for i in range(2):
            rows = slice(i * ROWS // 2, (i + 1) * ROWS // 2)
            cols = pl.ds(pl.multiple_of(j * PN, PN), PN)
            p_v[slot, rows, :] = jnp.dot(h_v[rows, :], wd[:, cols], preferred_element_type=F32).astype(BF)
        p_copy(j, slot).start()

    p_copy(D // PN - 2, 0).wait()
    p_copy(D // PN - 1, 1).wait()

    loads[4].wait()
    loads[5].wait()
    BN = 256

    def o_copies(j):
        cols = pl.ds(pl.multiple_of(j * BN, BN), BN)
        return (
            pltpu.make_async_copy(gate_v.at[:, cols], gg_out.at[:, cols], osem.at[0, j]),
            pltpu.make_async_copy(up_v.at[:, cols], ug_out.at[:, cols], osem.at[1, j]),
        )

    @pl.loop(0, HID // BN)
    def _(j):
        cols = pl.ds(pl.multiple_of(j * BN, BN), BN)
        for i in range(2):
            rows = slice(i * ROWS // 2, (i + 1) * ROWS // 2)
            gh = lax.dot_general(
                g_v[rows, :], wd[cols, :], (((1,), (1,)), ((), ())), preferred_element_type=F32
            )
            gate = gate_v[rows, cols].astype(F32)
            up = up_v[rows, cols].astype(F32)
            sig = jax.nn.sigmoid(gate)
            gate_v[rows, cols] = (gh * up * sig * (1.0 + gate * (1.0 - sig))).astype(BF)
            up_v[rows, cols] = (gh * gate * sig).astype(BF)
        for copy in o_copies(j):
            copy.start()

    @pl.loop(0, HID // BN)
    def _(j):
        for copy in o_copies(j):
            copy.wait()

    @pl.loop(0, N_DP)
    def _(o):
        @pl.loop(0, MAXB)
        def _(s):
            q_copy(o, s, zero_v).wait()


def add_rows(dst, sources, rows, step):
    @pl.loop(0, rows // step)
    def _(i):
        part = pl.ds(pl.multiple_of(i * step, step), step)
        total = sources[0][part, :].astype(F32)
        for source in sources[1:]:
            total = total + source[part, :].astype(F32)
        dst[part, :] = total.astype(dst.dtype)


def scatter_kernel(
    p_ref, q_ref, mixed_ref, bg_ref,
    pa, pb, po, prel, pm, pp, pz, qv, qc, qrel, qm, qp, qh,
    m_send, m_recv, q_send, q_recv, ploc, qloc,
):
    dp, t = lax.axis_index("dp"), lax.axis_index("tensor")
    z, yp, ym, y2 = flip_core(t), (t + 2) % N_T, (t + 6) % N_T, (t + 4) % N_T
    h, xp, xm = flip_far(dp), (dp + 4) % N_DP, (dp + 12) % N_DP
    c = flip_core(dp)
    Z, YP, YM = (dp, z), (dp, yp), (dp, ym)
    H, XP, XM, C = (h, t), (xp, t), (xm, t), (c, t)
    x, core = dp // 4, dp % 2
    xpi, xmi, x2i = (x + 1) % 4, (x + 3) % 4, (x + 2) % 4
    zh, zl = (dp // 2) % 2, t % 2
    ybase, ypb, ymb, y2b = t - zl, yp - zl, ym - zl, y2 - zl

    ploads = [
        pltpu.make_async_copy(p_ref.at[ypb], pa, ploc.at[0]),
        pltpu.make_async_copy(p_ref.at[ymb + 1], pb, ploc.at[1]),
        pltpu.make_async_copy(p_ref.at[ybase], po.at[0], ploc.at[2]),
        pltpu.make_async_copy(p_ref.at[ybase + 1], po.at[1], ploc.at[3]),
    ]
    order = [(x2i, 0), (x2i, 1), (xpi, 1), (xmi, 0), (xpi, 0), (xmi, 1), (x, 0), (x, 1)]
    qloads = [
        pltpu.make_async_copy(q_ref.at[(xi * 4 + p * 2) + core], qv.at[k], qloc.at[k])
        for k, (xi, p) in enumerate(order)
    ]
    for copy in qloads + ploads:
        copy.start()
    greet((Z, YP, YM, H, XP, XM, C))

    m, q = Sends(m_send, m_recv), Sends(q_send, q_recv)
    for k, (xi, p) in enumerate(order[:2]):
        q.start(7 + k, q_ref.at[(xi * 4 + p * 2) + 1 - core], qc.at[k], C)
    m.start(0, p_ref.at[y2b], prel.at[0], YP)
    m.start(1, p_ref.at[y2b + 1], prel.at[1], YM)
    m.start(2, p_ref.at[ypb + 1], pm.at[1], YP)
    m.start(3, p_ref.at[ymb], pp.at[0], YM)
    for k, (xi, p) in enumerate(order):
        if k >= 2:
            q.start(7 + k, q_ref.at[(xi * 4 + p * 2) + 1 - core], qc.at[k], C)

    def add_sibling(k, extra=()):
        q.arrived(7 + k, qc.at[k], C)
        qloads[k].wait()
        add_rows(qv.at[k], [qv.at[k], qc.at[k], *extra], PIECE, 208)

    add_sibling(0)
    q.start(0, qv.at[0], qrel.at[0], XP)
    add_sibling(1)
    q.start(1, qv.at[1], qrel.at[1], XM)
    add_sibling(2)
    q.start(2, qv.at[2], qm.at[1], XP)
    add_sibling(3)
    q.start(3, qv.at[3], qp.at[0], XM)

    q.arrived(0, qrel.at[0], XM)
    add_sibling(4, [qrel.at[0]])
    q.start(4, qv.at[4], qm.at[0], XP)
    q.arrived(1, qrel.at[1], XP)
    add_sibling(5, [qrel.at[1]])
    q.start(5, qv.at[5], qp.at[1], XM)

    ploads[0].wait()
    m.arrived(0, prel.at[0], YM)
    add_rows(pa, [pa, prel.at[0]], TOK, 16)
    m.start(4, pa, pm.at[0], YP)
    ploads[1].wait()
    m.arrived(1, prel.at[1], YP)
    add_rows(pb, [pb, prel.at[1]], TOK, 16)
    m.start(5, pb, pp.at[1], YM)

    for k in (6, 7):
        q.arrived(7 + k, qc.at[k], C)
        qloads[k].wait()
    q.arrived(2, qm.at[1], XM)
    q.arrived(3, qp.at[0], XP)
    q.arrived(4, qm.at[0], XM)
    q.arrived(5, qp.at[1], XP)
    add_rows(qv.at[7 - zh], [qv.at[7 - zh], qc.at[7 - zh], qm.at[1 - zh], qp.at[1 - zh]], PIECE, 208)
    q.start(6, qv.at[7 - zh], qh, H)

    ploads[2].wait()
    ploads[3].wait()
    m.arrived(2, pm.at[1], YM)
    m.arrived(3, pp.at[0], YP)
    m.arrived(4, pm.at[0], YM)
    m.arrived(5, pp.at[1], YP)
    add_rows(po.at[1 - zl], [po.at[1 - zl], pm.at[1 - zl], pp.at[1 - zl]], TOK, 16)
    m.start(6, po.at[1 - zl], pz, Z)

    q.arrived(6, qh, H)
    add_rows(bg_ref, [qv.at[6 + zh], qc.at[6 + zh], qm.at[zh], qp.at[zh], qh], PIECE, 208)
    m.arrived(6, pz, Z)
    add_rows(mixed_ref, [po.at[zl], pm.at[zl], pp.at[zl], pz], TOK, 16)
    m.finish()
    q.finish()


def local(gate_pre, up_pre, out_grad, w_blocks, block_ids):
    scale = 1.0 / math.sqrt(ROWS * N_DP)
    ids = block_ids[0, 0]
    meta = jnp.zeros((META, BLK), BF)
    meta = meta.at[0, :MAXB].set((ids // NDB).astype(BF)).at[1, :MAXB].set((ids % NDB).astype(BF))
    packed = jnp.concatenate([w_blocks.reshape(PIECE, BLK), meta], axis=0)

    sem = pltpu.SemaphoreType.DMA
    g_all, w_all, hid, hid_t = pl.pallas_call(
        gather_kernel,
        out_shape=(
            jax.ShapeDtypeStruct((N_T, TOK, D), BF),
            jax.ShapeDtypeStruct((N_DP, WROWS, BLK), BF),
            jax.ShapeDtypeStruct((ROWS, HID), BF),
            jax.ShapeDtypeStruct((HID, ROWS), BF),
        ),
        in_specs=[ANY] * 4,
        out_specs=[ANY] * 4,
        scratch_shapes=[
            pltpu.VMEM((ROWS, HID), BF),
            pltpu.VMEM((ROWS, HID), BF),
            pltpu.VMEM((ROWS, HID), BF),
            pltpu.VMEM((HID, ROWS), BF),
            sem((9,)), sem((9,)), sem((19,)), sem((19,)), sem((6,)),
        ],
        compiler_params=pltpu.CompilerParams(
            collective_id=0, has_side_effects=True, vmem_limit_bytes=40 * MIB
        ),
        name="gather",
    )(out_grad, packed, gate_pre, up_pre)

    parts, packed_grads, gate_grad, up_grad = pl.pallas_call(
        functools.partial(compute_kernel, scale),
        out_shape=(
            jax.ShapeDtypeStruct((ROWS, D), BF),
            jax.ShapeDtypeStruct((N_DP, PIECE, BLK), BF),
            jax.ShapeDtypeStruct((ROWS, HID), BF),
            jax.ShapeDtypeStruct((ROWS, HID), BF),
        ),
        in_specs=[ANY] * 6,
        out_specs=[ANY] * 4,
        scratch_shapes=[
            pltpu.VMEM((HID, D), BF),
            pltpu.VMEM((ROWS, HID), BF),
            pltpu.VMEM((HID, ROWS), BF),
            pltpu.VMEM((ROWS, D), BF),
            pltpu.VMEM((NLOC, BLK, BLK), BF),
            pltpu.VMEM((ROWS, HID), BF),
            pltpu.VMEM((ROWS, HID), BF),
            pltpu.VMEM((N_DP, META, BLK), BF),
            pltpu.VMEM((N_DP, BLK), jnp.int32),
            pltpu.SMEM((N_DP, BLK), jnp.int32),
            pltpu.VMEM((2, ROWS, 512), BF),
            pltpu.VMEM((BLK, BLK), BF),
            sem((7,)), sem, sem((2,)), sem, sem((2, 7)),
        ],
        compiler_params=pltpu.CompilerParams(vmem_limit_bytes=60 * MIB),
        name="compute",
    )(gate_pre, up_pre, hid, hid_t, g_all.reshape(ROWS, D), w_all)

    mixed, grads = pl.pallas_call(
        scatter_kernel,
        out_shape=(
            jax.ShapeDtypeStruct((TOK, D), BF),
            jax.ShapeDtypeStruct((PIECE, BLK), F32),
        ),
        in_specs=[ANY] * 2,
        out_specs=[VM] * 2,
        scratch_shapes=[
            pltpu.VMEM((TOK, D), BF),
            pltpu.VMEM((TOK, D), BF),
            pltpu.VMEM((2, TOK, D), BF),
            pltpu.VMEM((2, TOK, D), BF),
            pltpu.VMEM((2, TOK, D), BF),
            pltpu.VMEM((2, TOK, D), BF),
            pltpu.VMEM((TOK, D), BF),
            pltpu.VMEM((8, PIECE, BLK), BF),
            pltpu.VMEM((8, PIECE, BLK), BF),
            pltpu.VMEM((2, PIECE, BLK), BF),
            pltpu.VMEM((2, PIECE, BLK), BF),
            pltpu.VMEM((2, PIECE, BLK), BF),
            pltpu.VMEM((PIECE, BLK), BF),
            sem((7,)), sem((7,)), sem((15,)), sem((15,)), sem((4,)), sem((8,)),
        ],
        compiler_params=pltpu.CompilerParams(
            collective_id=1, has_side_effects=True, vmem_limit_bytes=56 * MIB
        ),
        name="scatter",
    )(parts.reshape(N_T, TOK, D), packed_grads)
    return mixed, gate_grad, up_grad, grads.reshape(1, 1, MAXB, BLK, BLK)


def solution(mesh):
    placed = (
        P("dp", "tensor"),
        P("dp", "tensor"),
        P(("dp", "tensor"), None),
        P("tensor", "dp", None, None, None),
        P("tensor", "dp", None),
    )
    return jax.shard_map(
        local,
        mesh=mesh,
        in_specs=placed,
        out_specs=(
            P(("dp", "tensor"), None),
            P("dp", "tensor"),
            P("dp", "tensor"),
            P("tensor", "dp", None, None, None),
        ),
        check_vma=False,
    )
```

time: 1160 us -> 284 us (0.24)
  local copies, waits for them, and re-layouts: 452 us -> 12.2 us
  matrix products: 373 us -> 0 us
  Pallas kernels: 0 us -> 269 us
  other arithmetic: 157 us -> 1.88 us
  waiting for transfers between devices: 135 us -> 0 us
  between operations: 14.6 us -> 0.69 us
  blocking collectives: 13.1 us -> 0 us
    dot_general x120 -> x0, matrix products: 373 us -> none  [the longest x28 142 us: forward_add_rank(): jnp.einsum('cta,cad->ctd', panel, weight_rank, preferred_element_type=jnp...]
    gather x129 -> x0, local copies, waits for them, and re-layouts: 270 us -> none  [the longest x64 149 us: backward_add_rank(): panel = jnp.take(grad_major, picks, axis=0)]
    pallas_call x0 -> x3, Pallas kernels: none -> 269 us  [the longest x1 107 us: local(): pl.pallas_call(scatter_kernel, out_shape=(jax.ShapeDtypeStruct((TOK, D),...]
    all_gather x2 -> x0, waiting for transfers between devices: 133 us -> none  [the longest x1 133 us: local(): piece = lax.all_gather(out_grad, 'tensor', axis=0, tiled=True)]
    while x33 -> x0, local copies, waits for them, and re-layouts: 75.4 us -> none  [the longest x5 35.6 us: blockwise_map(): result = lax.map(lambda grouped: func(*grouped), pieces)]
    add x4 -> x0, other arithmetic: 56.4 us -> none  [blockwise_sum(): running + func(*grouped)]
    dynamic_slice x32 -> x0, local copies, waits for them, and re-layouts: 49.6 us -> none  [the longest x24 30.5 us: blockwise_map(): result = lax.map(lambda grouped: func(*grouped), pieces)]
    reduce_and x64 -> x0, other arithmetic: 44.3 us -> none  [backward_add_rank(): panel = jnp.take(grad_major, picks, axis=0)]
  transfers between devices with their start and end apart: 4 -> 0, of which waited for: 1 -> 0; matrix products, arithmetic and copies ran while one was open for 85% -> 0% of each run, Pallas kernels for 0% -> 0%
where the time goes in v1:
time: 284 us; the launch traced here: 283 us
  Pallas kernels  269 us (95%)
  local copies, waits for them, and re-layouts  12.2 us (4%)
    pallas_call x1, Pallas kernels, local(): pl.pallas_call(scatter_kernel, out_shape=(jax.ShapeDtypeStruct((TOK, D),...  107 us
    pallas_call x1, Pallas kernels, local(): pl.pallas_call(gather_kernel, out_shape=(jax.ShapeDtypeStruct((N_T, TOK,...  83.6 us
    pallas_call x1, Pallas kernels, local(): pl.pallas_call(functools.partial(compute_kernel, scale), out_shape=(jax.S...  78.3 us
    unnamed x10, local copies, waits for them, and re-layouts  12 us

profile of v1, /device:TPU:1, one launch (start us, length us, event | category | flops | bytes accessed | tf_op | source)
XLA Modules:
  0.0 283.4 jit_solution(8417183337413571455)
XLA Ops:
  0.6 0.7 fusion
  1.3 0.2 scatter.12
  1.5 1.2 pad_maximum_fusion.w_ref
  2.7 0.0 copy-start
  2.7 2.0 copy-done
  4.7 0.0 copy-start.3
  4.7 1.2 copy-done.3
  6.0 83.6 %gather.1 = (bf16[8,128,4096]{2,1,0:T(8,128)(2,1)}, bf16[16,3344,128]{2,1,0:T(8,128)(2,1)}, bf16[1024,1792]{1,0:T(8,128)(2,1)S(1)}, bf16[1792,1024]{1,0:T(8,128)(2,1)S(1)}) custom-call(bf16[128,4096]{1,0:T(8,128)(2,1)S(1)} %copy-done.3, bf16[3344,128]{1,0:T(8,128)(2,1)S(1)} %pad_maximum_fusion.w_ref, bf16[1024,1792]{1,0:T(8,128)(2,1)S(1)} %copy-done, ...), custom_call_target="tpu_custom_call" | custom-call | tf_op jit(solution)/shard_map/gather/pallas_call | solution.py:457
  89.5 0.0 copy-start.1
  89.5 1.9 copy-done.1
  91.4 0.0 copy-start.2
  91.4 1.8 copy-done.2
  93.2 78.3 %compute.1 = (bf16[1024,4096]{1,0:T(8,128)(2,1)}, bf16[16,3328,128]{2,1,0:T(8,128)(2,1)}, bf16[1024,1792]{1,0:T(8,128)(2,1)}, bf16[1024,1792]{1,0:T(8,128)(2,1)}) custom-call(bf16[1024,1792]{1,0:T(8,128)(2,1)} %gate_ref.3, bf16[1024,1792]{1,0:T(8,128)(2,1)} %up_ref.3, bf16[1024,1792]{1,0:T(8,128)(2,1)} %copy-done.1, bf16[1792,1024]{1,0:T(8,128)(2,1)} %copy-done.2, ...), custom_call_target="tpu_custom_call" | custom-call | tf_op jit(solution)/shard_map/compute/pallas_call | solution.py:480
  171.6 106.7 %scatter.13 = (bf16[128,4096]{1,0:T(8,128)(2,1)}, f32[3328,128]{1,0:T(8,128)}) custom-call(bf16[8,128,4096]{2,1,0:T(8,128)(2,1)} %bitcast.21, bf16[16,3328,128]{2,1,0:T(8,128)(2,1)} %get-tuple-element.43.q_ref), custom_call_target="tpu_custom_call" | custom-call | tf_op jit(solution)/shard_map/scatter/pallas_call | solution.py:509
  278.3 2.3 copy.12
  280.6 2.8 copy.13
  (1 shorter events, 0.0 us)
Async XLA Ops:
  2.7 2.0 copy-start
  4.7 1.2 copy-start.3
  89.5 1.9 copy-start.1
  91.4 1.8 copy-start.2

commit v2 on v1

v2 whole, which is shorter than its diff:
```python
import functools
import math

import jax
import jax.numpy as jnp
from jax import lax
from jax.experimental import pallas as pl
from jax.experimental.pallas import tpu as pltpu
from jax.sharding import PartitionSpec as P

MESH = pl.DeviceIdType.MESH
BF = jnp.bfloat16
F32 = jnp.float32
ANY = pl.BlockSpec(memory_space=pl.ANY)
VM = pl.BlockSpec(memory_space=pltpu.VMEM)
MIB = 1024 * 1024

N_DP = 16
N_T = 8
BLK = 128
TOK = 128
NFB = 14
NDB = 32
NLOC = NFB * NDB
MAXB = 26
D = NDB * BLK
HID = NFB * BLK
ROWS = TOK * N_T
PIECE = MAXB * BLK
META = 16
WROWS = PIECE + META
WHALF = 1680


def flip_core(i):
    return i + 1 - 2 * (i % 2)


def flip_far(i):
    return i + 2 - 4 * ((i // 2) % 2)


def greet(devices):
    barrier = pltpu.get_barrier_semaphore()
    for device in devices:
        pl.semaphore_signal(barrier, inc=1, device_id=device, device_id_type=MESH)
    pl.semaphore_wait(barrier, len(devices))


class Sends:
    def __init__(self, send, recv):
        self.send, self.recv, self.started = send, recv, []

    def start(self, i, src, dst, device):
        copy = pltpu.make_async_remote_copy(
            src, dst, self.send.at[i], self.recv.at[i], device_id=device, device_id_type=MESH
        )
        copy.start()
        self.started.append(copy)

    def arrived(self, i, dst, device):
        pltpu.make_async_remote_copy(
            dst, dst, self.send.at[i], self.recv.at[i], device_id=device, device_id_type=MESH
        ).wait_recv()

    def finish(self):
        for copy in self.started:
            copy.wait_send()


def gather_kernel(
    g_ref, w_ref, gate_ref, up_ref, g_all, w_all, h_out, ht_out,
    gate_v, up_v, h_v, ht_v, g_send, g_recv, w_send, w_recv, loc,
):
    dp, t = lax.axis_index("dp"), lax.axis_index("tensor")
    z, yp, ym, y2 = flip_core(t), (t + 2) % N_T, (t + 6) % N_T, (t + 4) % N_T
    h, xp, xm, x2 = flip_far(dp), (dp + 4) % N_DP, (dp + 12) % N_DP, (dp + 8) % N_DP
    c = flip_core(dp)
    Z, YP, YM = (dp, z), (dp, yp), (dp, ym)
    H, XP, XM, C = (h, t), (xp, t), (xm, t), (c, t)

    local = [
        pltpu.make_async_copy(gate_ref, gate_v, loc.at[0]),
        pltpu.make_async_copy(up_ref, up_v, loc.at[1]),
        pltpu.make_async_copy(g_ref, g_all.at[t], loc.at[2]),
        pltpu.make_async_copy(w_ref, w_all.at[dp], loc.at[3]),
    ]
    for copy in local:
        copy.start()
    greet((Z, YP, YM, H, XP, XM, C))

    g, w = Sends(g_send, g_recv), Sends(w_send, w_recv)
    lo, hi = pl.ds(0, TOK // 2), pl.ds(TOK // 2, TOK // 2)
    first, mid_lo, mid_hi, last = pl.ds(0, 16), pl.ds(16, 48), pl.ds(64, 48), pl.ds(112, 16)
    wlo, whi = pl.ds(0, WHALF), pl.ds(WHALF, WROWS - WHALF)

    g.start(0, g_ref, g_all.at[t], Z)
    w.start(0, w_ref, w_all.at[dp], H)
    g.start(1, g_ref, g_all.at[t], YP)
    g.start(2, g_ref, g_all.at[t], YM)
    w.start(1, w_ref, w_all.at[dp], XP)
    w.start(2, w_ref, w_all.at[dp], XM)
    w.start(9, w_ref, w_all.at[dp], C)

    local[0].wait()
    local[1].wait()

    @pl.loop(0, ROWS // TOK)
    def _(i):
        rows = pl.ds(pl.multiple_of(i * TOK, TOK), TOK)
        for b in range(NFB):
            cols = pl.ds(b * BLK, BLK)
            gate = gate_v[rows, cols].astype(F32)
            hid = (gate * jax.nn.sigmoid(gate) * up_v[rows, cols].astype(F32)).astype(BF)
            h_v[rows, cols] = hid
            ht_v[cols, rows] = hid.T

    outs = [
        pltpu.make_async_copy(h_v, h_out, loc.at[4]),
        pltpu.make_async_copy(ht_v, ht_out, loc.at[5]),
    ]
    for copy in outs:
        copy.start()

    w.arrived(1, w_all.at[xm], XM)
    w.start(5, w_all.at[xm, wlo], w_all.at[xm, wlo], XP)
    w.start(11, w_all.at[xm], w_all.at[xm], C)
    w.arrived(2, w_all.at[xp], XP)
    w.start(6, w_all.at[xp, whi], w_all.at[xp, whi], XM)
    w.start(12, w_all.at[xp], w_all.at[xp], C)

    g.arrived(1, g_all.at[ym], YM)
    g.start(5, g_all.at[ym, lo], g_all.at[ym, lo], YP)
    g.arrived(2, g_all.at[yp], YP)
    g.start(6, g_all.at[yp, hi], g_all.at[yp, hi], YM)
    g.arrived(0, g_all.at[z], Z)
    g.start(3, g_all.at[z], g_all.at[z], YP)
    g.start(4, g_all.at[z], g_all.at[z], YM)

    w.arrived(0, w_all.at[h], H)
    w.start(3, w_all.at[h], w_all.at[h], XP)
    w.start(4, w_all.at[h], w_all.at[h], XM)
    w.start(10, w_all.at[h], w_all.at[h], C)

    w.arrived(5, w_all.at[x2, wlo], XM)
    w.start(15, w_all.at[x2, wlo], w_all.at[x2, wlo], C)
    w.arrived(6, w_all.at[x2, whi], XP)
    w.start(16, w_all.at[x2, whi], w_all.at[x2, whi], C)

    zm, zp, z2 = flip_core(ym), flip_core(yp), flip_core(y2)
    g.arrived(5, g_all.at[y2, lo], YM)
    g.start(9, g_all.at[y2, mid_lo], g_all.at[y2, mid_lo], Z)
    g.arrived(6, g_all.at[y2, hi], YP)
    g.start(10, g_all.at[y2, mid_hi], g_all.at[y2, mid_hi], Z)
    g.arrived(3, g_all.at[zm], YM)
    g.start(7, g_all.at[zm, first], g_all.at[zm, first], YP)
    g.arrived(4, g_all.at[zp], YP)
    g.start(8, g_all.at[zp, last], g_all.at[zp, last], YM)

    hm, hp, h2 = flip_far(xm), flip_far(xp), flip_far(x2)
    w.arrived(3, w_all.at[hm], XM)
    w.start(7, w_all.at[hm, wlo], w_all.at[hm, wlo], XP)
    w.start(13, w_all.at[hm], w_all.at[hm], C)
    w.arrived(4, w_all.at[hp], XP)
    w.start(8, w_all.at[hp, whi], w_all.at[hp, whi], XM)
    w.start(14, w_all.at[hp], w_all.at[hp], C)
    w.arrived(7, w_all.at[h2, wlo], XM)
    w.start(17, w_all.at[h2, wlo], w_all.at[h2, wlo], C)
    w.arrived(8, w_all.at[h2, whi], XP)
    w.start(18, w_all.at[h2, whi], w_all.at[h2, whi], C)

    g.arrived(7, g_all.at[z2, first], YM)
    g.arrived(8, g_all.at[z2, last], YP)
    g.arrived(9, g_all.at[z2, mid_lo], Z)
    g.arrived(10, g_all.at[z2, mid_hi], Z)
    for i, source in ((9, dp), (10, h), (11, xm), (12, xp), (13, hm), (14, hp)):
        w.arrived(i, w_all.at[flip_core(source)], C)
    for i, source, part in ((15, x2, wlo), (16, x2, whi), (17, h2, wlo), (18, h2, whi)):
        w.arrived(i, w_all.at[flip_core(source), part], C)
    g.finish()
    w.finish()
    for copy in (local[2], local[3], outs[0], outs[1]):
        copy.wait()


def weight_kernel(
    scale, ht_ref, g_ref, w_ref, q_out, wd_out,
    wd, ht_v, g_v, blocks, meta_v, ids_v, ids_s, zero_v, loc, wsem, qsem,
):
    loads = [
        pltpu.make_async_copy(w_ref.at[:, pl.ds(PIECE, META)], meta_v, loc.at[0]),
        pltpu.make_async_copy(ht_ref, ht_v, loc.at[1]),
        pltpu.make_async_copy(g_ref, g_v, loc.at[2]),
    ]
    for copy in loads:
        copy.start()

    @pl.loop(0, HID // 16)
    def _(i):
        wd[pl.ds(pl.multiple_of(i * 16, 16), 16), :] = jnp.zeros((16, D), BF)

    zero_v[...] = jnp.zeros((BLK, BLK), BF)
    loads[0].wait()
    for o in range(N_DP):
        both = meta_v[o].astype(F32)
        ids_v[o : o + 1, :] = (both[0:1, :] * NDB + both[1:2, :]).astype(jnp.int32)
    to_scalar = pltpu.make_async_copy(ids_v, ids_s, loc.at[3])
    to_scalar.start()
    to_scalar.wait()

    def w_copy(o, s):
        b = ids_s[o, s]
        row = pl.multiple_of((b // NDB) * BLK, BLK)
        col = pl.multiple_of((b % NDB) * BLK, BLK)
        src = w_ref.at[o, pl.ds(pl.multiple_of(s * BLK, BLK), BLK), :]
        return b, pltpu.make_async_copy(src, wd.at[pl.ds(row, BLK), pl.ds(col, BLK)], wsem)

    @pl.loop(0, N_DP)
    def _(o):
        @pl.loop(0, MAXB)
        def _(s):
            b, copy = w_copy(o, s)

            @pl.when(b < NLOC)
            def _():
                copy.start()

    loads[1].wait()
    loads[2].wait()
    TN = 512

    @pl.loop(0, D // TN)
    def _(j):
        for i in range(2):
            rows = HID // 2
            cols = pl.ds(pl.multiple_of(j * TN, TN), TN)
            res = jnp.dot(ht_v[i * rows : (i + 1) * rows, :], g_v[:, cols], preferred_element_type=F32)
            res = (res * scale).astype(BF)
            for cb in range(TN // BLK):
                for rb in range(NFB // 2):
                    blocks[(j * (TN // BLK) + cb) * NFB + i * (NFB // 2) + rb] = res[
                        rb * BLK : (rb + 1) * BLK, cb * BLK : (cb + 1) * BLK
                    ]

    def q_copy(o, s, src):
        dst = q_out.at[o, pl.ds(pl.multiple_of(s * BLK, BLK), BLK), :]
        return pltpu.make_async_copy(src, dst, qsem)

    @pl.loop(0, N_DP)
    def _(o):
        @pl.loop(0, MAXB)
        def _(s):
            b, copy = w_copy(o, s)

            @pl.when(b < NLOC)
            def _():
                copy.wait()
                q_copy(o, s, blocks.at[(b % NDB) * NFB + b // NDB]).start()

            @pl.when(b >= NLOC)
            def _():
                q_copy(o, s, zero_v).start()

    dense = pltpu.make_async_copy(wd, wd_out, loc.at[4])
    dense.start()

    @pl.loop(0, N_DP)
    def _(o):
        @pl.loop(0, MAXB)
        def _(s):
            q_copy(o, s, zero_v).wait()

    dense.wait()


def add_rows(dst, sources, rows, step):
    @pl.loop(0, rows // step)
    def _(i):
        part = pl.ds(pl.multiple_of(i * step, step), step)
        total = sources[0][part, :].astype(F32)
        for source in sources[1:]:
            total = total + source[part, :].astype(F32)
        dst[part, :] = total.astype(dst.dtype)


NCH = 8
CW = D // NCH
NSP = 2
SR = PIECE // NSP
BN = 256
NBW = HID // BN
QSLOTS = 8


def scatter_kernel(
    gate_ref, up_ref, h_ref, wd_ref, g_ref, q_ref, mixed_ref, bg_ref, gg_out, ug_out,
    h_v, wd, g_v, gate_v, up_v, pv, prel, pm, pp, pz, qv, qc, qrel, qm, qp, qh,
    m_send, m_recv, q_send, q_recv, loc, wloc, qloc, bloc, oloc,
):
    dp, t = lax.axis_index("dp"), lax.axis_index("tensor")
    z, yp, ym, y2 = flip_core(t), (t + 2) % N_T, (t + 6) % N_T, (t + 4) % N_T
    h, xp, xm = flip_far(dp), (dp + 4) % N_DP, (dp + 12) % N_DP
    c = flip_core(dp)
    Z, YP, YM = (dp, z), (dp, yp), (dp, ym)
    H, XP, XM, C = (h, t), (xp, t), (xm, t), (c, t)
    x, core = dp // 4, dp % 2
    xpi, xmi, x2i = (x + 1) % 4, (x + 3) % 4, (x + 2) % 4
    zh, zl = (dp // 2) % 2, t % 2
    ypb, ymb, y2b = yp - zl, ym - zl, y2 - zl

    pieces = [(x2i, 0), (x2i, 1), (xpi, 1), (xmi, 0), (xpi, 0), (xmi, 1), (x, 0), (x, 1)]
    order = [(0, 0), (1, 0), (0, 1), (1, 1), (2, 0), (3, 0), (4, 0), (5, 0)]
    order += [(2, 1), (3, 1), (4, 1), (5, 1), (6, 0), (7, 0), (6, 1), (7, 1)]
    place = {item: i for i, item in enumerate(order)}

    def q_load(i):
        k, s = order[i]
        xi, p = pieces[k]
        src = q_ref.at[(xi * 4 + p * 2) + core, pl.ds(s * SR, SR)]
        return pltpu.make_async_copy(src, qv.at[i % QSLOTS], qloc.at[i])

    def w_load(k):
        cols = pl.ds(k * CW, CW)
        return pltpu.make_async_copy(wd_ref.at[:, cols], wd.at[:, cols], wloc.at[k])

    h_load = pltpu.make_async_copy(h_ref, h_v, loc.at[0])
    g_load = pltpu.make_async_copy(g_ref, g_v, loc.at[1])
    for i in range(4):
        q_load(i).start()
    h_load.start()
    for k in range(NCH):
        w_load(k).start()
    for i in range(4, QSLOTS):
        q_load(i).start()
    greet((Z, YP, YM, H, XP, XM, C))

    m, q = Sends(m_send, m_recv), Sends(q_send, q_recv)
    for k, s in order:
        xi, p = pieces[k]
        src = q_ref.at[(xi * 4 + p * 2) + 1 - core, pl.ds(s * SR, SR)]
        q.start(14 + place[k, s], src, qc.at[k, s], C)

    def add_sibling(k, s, extra=()):
        i = place[k, s]
        q.arrived(14 + i, qc.at[k, s], C)
        q_load(i).wait()
        add_rows(qc.at[k, s], [qv.at[i % QSLOTS], qc.at[k, s], *extra], SR, 208)
        if i + QSLOTS < len(order):
            q_load(i + QSLOTS).start()

    def q_relay(s):
        add_sibling(0, s)
        q.start(s, qc.at[0, s], qrel.at[0, s], XP)
        add_sibling(1, s)
        q.start(2 + s, qc.at[1, s], qrel.at[1, s], XM)

    def q_direct(s):
        add_sibling(2, s)
        q.start(4 + s, qc.at[2, s], qm.at[1, s], XP)
        add_sibling(3, s)
        q.start(6 + s, qc.at[3, s], qp.at[0, s], XM)

    def q_forward(s):
        q.arrived(s, qrel.at[0, s], XM)
        add_sibling(4, s, [qrel.at[0, s]])
        q.start(8 + s, qc.at[4, s], qm.at[0, s], XP)
        q.arrived(2 + s, qrel.at[1, s], XP)
        add_sibling(5, s, [qrel.at[1, s]])
        q.start(10 + s, qc.at[5, s], qp.at[1, s], XM)

    def q_far(s):
        add_sibling(6, s)
        add_sibling(7, s)
        q.arrived(4 + s, qm.at[1, s], XM)
        q.arrived(6 + s, qp.at[0, s], XP)
        q.arrived(8 + s, qm.at[0, s], XM)
        q.arrived(10 + s, qp.at[1, s], XP)
        mine = qc.at[7 - zh, s]
        add_rows(mine, [mine, qm.at[1 - zh, s], qp.at[1 - zh, s]], SR, 208)
        q.start(12 + s, mine, qh.at[s], H)

    def q_final(s):
        q.arrived(12 + s, qh.at[s], H)
        total = bg_ref.at[pl.ds(s * SR, SR)]
        add_rows(total, [qc.at[6 + zh, s], qm.at[zh, s], qp.at[zh, s], qh.at[s]], SR, 208)

    def part(k, tt):
        return pv.at[k, pl.ds(pl.multiple_of(tt * TOK, TOK), TOK)]

    def forward(k):
        w_load(k).wait()

        @pl.loop(0, 2)
        def _(i):
            rows = pl.ds(pl.multiple_of(i * (ROWS // 2), ROWS // 2), ROWS // 2)
            pv[k, rows, :] = jnp.dot(
                h_v[rows, :], wd[:, k * CW : (k + 1) * CW], preferred_element_type=F32
            ).astype(BF)

        m.start(7 * k, part(k, y2b), prel.at[0, k], YP)
        m.start(7 * k + 1, part(k, y2b + 1), prel.at[1, k], YM)

    def m_forward(k):
        m.arrived(7 * k, prel.at[0, k], YM)
        add_rows(part(k, ypb), [part(k, ypb), prel.at[0, k]], TOK, 64)
        m.start(7 * k + 4, part(k, ypb), pm.at[0, k], YP)
        m.arrived(7 * k + 1, prel.at[1, k], YP)
        add_rows(part(k, ymb + 1), [part(k, ymb + 1), prel.at[1, k]], TOK, 64)
        m.start(7 * k + 5, part(k, ymb + 1), pp.at[1, k], YM)
        m.start(7 * k + 2, part(k, ypb + 1), pm.at[1, k], YP)
        m.start(7 * k + 3, part(k, ymb), pp.at[0, k], YM)

    def m_near(k):
        m.arrived(7 * k + 4, pm.at[0, k], YM)
        m.arrived(7 * k + 5, pp.at[1, k], YP)
        m.arrived(7 * k + 2, pm.at[1, k], YM)
        m.arrived(7 * k + 3, pp.at[0, k], YP)
        mine = part(k, z)
        add_rows(mine, [mine, pm.at[1 - zl, k], pp.at[1 - zl, k]], TOK, 64)
        m.start(7 * k + 6, mine, pz.at[k], Z)

    def m_final(k):
        m.arrived(7 * k + 6, pz.at[k], Z)
        total = mixed_ref.at[:, pl.ds(k * CW, CW)]
        add_rows(total, [part(k, t), pm.at[zl, k], pp.at[zl, k], pz.at[k]], TOK, 64)

    def b_loads(j):
        cols = pl.ds(j * BN, BN)
        return (
            pltpu.make_async_copy(gate_ref.at[:, cols], gate_v.at[j % 2], bloc.at[0, j]),
            pltpu.make_async_copy(up_ref.at[:, cols], up_v.at[j % 2], bloc.at[1, j]),
        )

    def b_stores(j):
        cols = pl.ds(j * BN, BN)
        return (
            pltpu.make_async_copy(gate_v.at[j % 2], gg_out.at[:, cols], oloc.at[0, j]),
            pltpu.make_async_copy(up_v.at[j % 2], ug_out.at[:, cols], oloc.at[1, j]),
        )

    def backward(j):
        if j == 0:
            g_load.wait()
        if j >= 1:
            for copy in b_stores(j - 1):
                copy.wait()
        if j + 1 < NBW:
            for copy in b_loads(j + 1):
                copy.start()
        for copy in b_loads(j):
            copy.wait()

        @pl.loop(0, 2)
        def _(i):
            rows = pl.ds(pl.multiple_of(i * (ROWS // 2), ROWS // 2), ROWS // 2)
            gh = lax.dot_general(
                g_v[rows, :], wd[j * BN : (j + 1) * BN, :], (((1,), (1,)), ((), ())),
                preferred_element_type=F32,
            )
            gate = gate_v[j % 2, rows, :].astype(F32)
            up = up_v[j % 2, rows, :].astype(F32)
            sig = jax.nn.sigmoid(gate)
            gate_v[j % 2, rows, :] = (gh * up * sig * (1.0 + gate * (1.0 - sig))).astype(BF)
            up_v[j % 2, rows, :] = (gh * gate * sig).astype(BF)

        for copy in b_stores(j):
            copy.start()

    q_relay(0)
    q_relay(1)
    h_load.wait()
    g_load.start()
    for copy in b_loads(0):
        copy.start()
    forward(0)
    q_direct(0)
    forward(1)
    m_forward(0)
    q_forward(0)
    forward(2)
    m_forward(1)
    forward(3)
    m_forward(2)
    q_direct(1)
    forward(4)
    m_forward(3)
    q_forward(1)
    for k in range(5, NCH):
        forward(k)
        m_forward(k - 1)
    m_forward(NCH - 1)
    m_near(0)
    m_near(1)
    m_near(2)
    backward(0)
    backward(1)
    m_near(3)
    q_far(0)
    backward(2)
    backward(3)
    backward(4)
    m_near(4)
    m_final(0)
    m_final(1)
    backward(5)
    m_near(5)
    backward(6)
    q_final(0)
    q_far(1)
    for k in range(2, 6):
        m_final(k)
    m_near(6)
    m_near(7)
    q_final(1)
    m_final(6)
    m_final(7)
    m.finish()
    q.finish()
    for copy in b_stores(NBW - 1):
        copy.wait()


def local(gate_pre, up_pre, out_grad, w_blocks, block_ids):
    scale = 1.0 / math.sqrt(ROWS * N_DP)
    ids = block_ids[0, 0]
    meta = jnp.zeros((META, BLK), BF)
    meta = meta.at[0, :MAXB].set((ids // NDB).astype(BF)).at[1, :MAXB].set((ids % NDB).astype(BF))
    packed = jnp.concatenate([w_blocks.reshape(PIECE, BLK), meta], axis=0)

    sem = pltpu.SemaphoreType.DMA
    g_all, w_all, hid, hid_t = pl.pallas_call(
        gather_kernel,
        out_shape=(
            jax.ShapeDtypeStruct((N_T, TOK, D), BF),
            jax.ShapeDtypeStruct((N_DP, WROWS, BLK), BF),
            jax.ShapeDtypeStruct((ROWS, HID), BF),
            jax.ShapeDtypeStruct((HID, ROWS), BF),
        ),
        in_specs=[ANY] * 4,
        out_specs=[ANY] * 4,
        scratch_shapes=[
            pltpu.VMEM((ROWS, HID), BF),
            pltpu.VMEM((ROWS, HID), BF),
            pltpu.VMEM((ROWS, HID), BF),
            pltpu.VMEM((HID, ROWS), BF),
            sem((11,)), sem((11,)), sem((19,)), sem((19,)), sem((6,)),
        ],
        compiler_params=pltpu.CompilerParams(
            collective_id=0, has_side_effects=True, vmem_limit_bytes=60 * MIB
        ),
        name="gather",
    )(out_grad, packed, gate_pre, up_pre)

    packed_grads, dense = pl.pallas_call(
        functools.partial(weight_kernel, scale),
        out_shape=(
            jax.ShapeDtypeStruct((N_DP, PIECE, BLK), BF),
            jax.ShapeDtypeStruct((HID, D), BF),
        ),
        in_specs=[ANY] * 3,
        out_specs=[ANY] * 2,
        scratch_shapes=[
            pltpu.VMEM((HID, D), BF),
            pltpu.VMEM((HID, ROWS), BF),
            pltpu.VMEM((ROWS, D), BF),
            pltpu.VMEM((NLOC, BLK, BLK), BF),
            pltpu.VMEM((N_DP, META, BLK), BF),
            pltpu.VMEM((N_DP, BLK), jnp.int32),
            pltpu.SMEM((N_DP, BLK), jnp.int32),
            pltpu.VMEM((BLK, BLK), BF),
            sem((5,)), sem, sem,
        ],
        compiler_params=pltpu.CompilerParams(vmem_limit_bytes=60 * MIB),
        name="weight",
    )(hid_t, g_all.reshape(ROWS, D), w_all)

    mixed, grads, gate_grad, up_grad = pl.pallas_call(
        scatter_kernel,
        out_shape=(
            jax.ShapeDtypeStruct((TOK, D), BF),
            jax.ShapeDtypeStruct((PIECE, BLK), F32),
            jax.ShapeDtypeStruct((ROWS, HID), BF),
            jax.ShapeDtypeStruct((ROWS, HID), BF),
        ),
        in_specs=[ANY] * 6,
        out_specs=[VM, VM, ANY, ANY],
        scratch_shapes=[
            pltpu.VMEM((ROWS, HID), BF),
            pltpu.VMEM((HID, D), BF),
            pltpu.VMEM((ROWS, D), BF),
            pltpu.VMEM((2, ROWS, BN), BF),
            pltpu.VMEM((2, ROWS, BN), BF),
            pltpu.VMEM((NCH, ROWS, CW), BF),
            pltpu.VMEM((2, NCH, TOK, CW), BF),
            pltpu.VMEM((2, NCH, TOK, CW), BF),
            pltpu.VMEM((2, NCH, TOK, CW), BF),
            pltpu.VMEM((NCH, TOK, CW), BF),
            pltpu.VMEM((QSLOTS, SR, BLK), BF),
            pltpu.VMEM((8, NSP, SR, BLK), BF),
            pltpu.VMEM((2, NSP, SR, BLK), BF),
            pltpu.VMEM((2, NSP, SR, BLK), BF),
            pltpu.VMEM((2, NSP, SR, BLK), BF),
            pltpu.VMEM((NSP, SR, BLK), BF),
            sem((7 * NCH,)), sem((7 * NCH,)), sem((30,)), sem((30,)),
            sem((2,)), sem((NCH,)), sem((16,)), sem((2, NBW)), sem((2, NBW)),
        ],
        compiler_params=pltpu.CompilerParams(
            collective_id=1, has_side_effects=True, vmem_limit_bytes=63 * MIB
        ),
        name="scatter",
    )(gate_pre, up_pre, hid, dense, g_all.reshape(ROWS, D), packed_grads)
    return mixed, gate_grad, up_grad, grads.reshape(1, 1, MAXB, BLK, BLK)


def solution(mesh):
    placed = (
        P("dp", "tensor"),
        P("dp", "tensor"),
        P(("dp", "tensor"), None),
        P("tensor", "dp", None, None, None),
        P("tensor", "dp", None),
    )
    return jax.shard_map(
        local,
        mesh=mesh,
        in_specs=placed,
        out_specs=(
            P(("dp", "tensor"), None),
            P("dp", "tensor"),
            P("dp", "tensor"),
            P("tensor", "dp", None, None, None),
        ),
        check_vma=False,
    )
```

time: 284 us -> 251 us (0.88)
  Pallas kernels: 269 us -> 236 us
    pallas_call x1, Pallas kernels: 78.3 us -> 39.8 us  [local(): pl.pallas_call(functools.partial(weight_kernel, scale), out_shape=(jax.Sh...]
    pallas_call x1, Pallas kernels: 107 us -> 113 us  [local(): pl.pallas_call(scatter_kernel, out_shape=(jax.ShapeDtypeStruct((TOK, D),...]
    unnamed x10 -> x8, local copies, waits for them, and re-layouts: 12 us -> 10.4 us
where the time goes in v2:
time: 251 us; the launch traced here: 250 us
  Pallas kernels  236 us (94%)
  local copies, waits for them, and re-layouts  10.6 us (4%)
  other arithmetic  2.78 us (1%)
    pallas_call x1, Pallas kernels, local(): pl.pallas_call(scatter_kernel, out_shape=(jax.ShapeDtypeStruct((TOK, D),...  113 us
    pallas_call x1, Pallas kernels, local(): pl.pallas_call(gather_kernel, out_shape=(jax.ShapeDtypeStruct((N_T, TOK,...  83.5 us
    pallas_call x1, Pallas kernels, local(): pl.pallas_call(functools.partial(weight_kernel, scale), out_shape=(jax.Sh...  39.8 us
    unnamed x8, local copies, waits for them, and re-layouts  10.4 us

profile of v2, /device:TPU:1, one launch (start us, length us, event | category | flops | bytes accessed | tf_op | source)
XLA Modules:
  0.0 250.3 jit_solution(7944310597198263351)
XLA Ops:
  0.6 0.7 fusion
  1.3 0.2 scatter.12
  1.5 2.1 pad_maximum_fusion.w_ref
  3.6 83.5 %gather.1 = (bf16[8,128,4096]{2,1,0:T(8,128)(2,1)}, bf16[16,3344,128]{2,1,0:T(8,128)(2,1)}, bf16[1024,1792]{1,0:T(8,128)(2,1)}, bf16[1792,1024]{1,0:T(8,128)(2,1)}) custom-call(bf16[128,4096]{1,0:T(8,128)(2,1)} %g_ref.1, bf16[3344,128]{1,0:T(8,128)(2,1)} %pad_maximum_fusion.w_ref, bf16[1024,1792]{1,0:T(8,128)(2,1)} %gate_ref.3, bf16[1024,1792]{1,0:T(8,128)(2,1)} %up_ref.3), custom_call_target="tpu_custom_call" | custom-call | tf_op jit(solution)/shard_map/gather/pallas_call | solution.py:531
  87.1 39.8 %weight.1 = (bf16[16,3328,128]{2,1,0:T(8,128)(2,1)}, bf16[1792,4096]{1,0:T(8,128)(2,1)}) custom-call(bf16[1792,1024]{1,0:T(8,128)(2,1)} %get-tuple-element.39.ht_ref, bf16[1024,4096]{1,0:T(8,128)(2,1)} %bitcast.20, bf16[16,3344,128]{2,1,0:T(8,128)(2,1)} %get-tuple-element.41.w_ref), custom_call_target="tpu_custom_call" | custom-call | tf_op jit(solution)/shard_map/weight/pallas_call | solution.py:554
  126.9 112.9 %scatter.13 = (bf16[128,4096]{1,0:T(8,128)(2,1)}, f32[3328,128]{1,0:T(8,128)}, bf16[1024,1792]{1,0:T(8,128)(2,1)}, bf16[1024,1792]{1,0:T(8,128)(2,1)}) custom-call(bf16[1024,1792]{1,0:T(8,128)(2,1)} %gate_ref.3, bf16[1024,1792]{1,0:T(8,128)(2,1)} %up_ref.3, bf16[1024,1792]{1,0:T(8,128)(2,1)} %get-tuple-element.38.h_ref, ...), custom_call_target="tpu_custom_call" | custom-call | tf_op jit(solution)/shard_map/scatter/pallas_call | solution.py:577
  239.8 2.3 copy.14
  242.1 0.0 copy-start
  242.1 4.3 %copy.15 = bf16[1024,1792]{1,0:T(8,128)(2,1)} copy(bf16[1024,1792]{1,0:T(8,128)(2,1)} %get-tuple-element.55) | data formatting | bytes 7340032
  246.4 0.0 copy-done
  246.4 0.0 copy-start.1
  246.4 1.8 copy.16
  248.2 0.8 copy-done.1
  249.1 1.2 copy.17
  (1 shorter events, 0.0 us)
Async XLA Ops:
  242.1 4.3 %copy-start = (bf16[1024,1792]{1,0:T(8,128)(2,1)S(1)}, bf16[1024,1792]{1,0:T(8,128)(2,1)}, u32[]{:S(2)}) copy-start(bf16[1024,1792]{1,0:T(8,128)(2,1)} %get-tuple-element.56) | copy-start | bytes 11010052
  246.4 2.7 %copy-start.1 = (f32[3328,128]{1,0:T(8,128)S(1)}, f32[3328,128]{1,0:T(8,128)}, u32[]{:S(2)}) copy-start(f32[3328,128]{1,0:T(8,128)} %get-tuple-element.47) | copy-start | bytes 5111812
